TPU v7x, 32 devices: a whole 2x2x4 slice. The times are simulated.
32 devices in a mesh: parts: 1, ctx: 4 (over z), pb: 4 (over y, x), row: 2 (over core).
Axes of the slice: x: 2, y: 2, z: 4, core: 2. Of those that a mesh axis runs over, the one named last changes fastest.
Arguments:
- queries: bfloat16 [2048, 3072], P(('parts', 'ctx', 'pb', 'row')), may hold values from -10 to 10
- cache_keys: bfloat16 [4096, 192], P(('parts', 'ctx')), may hold values from -10 to 10
- cache_values: bfloat16 [4096, 128], P(('parts', 'ctx')), may hold values from -6 to 6
- span_keys: bfloat16 [2048, 192], P(('parts', 'ctx')), may hold values from -10 to 10
- span_values: bfloat16 [2048, 128], P(('parts', 'ctx')), may hold values from -6 to 6
- pool_keys: float32 [32, 192], replicated, may hold values from 0.2 to 0.6
- pool_values: float32 [32, 128], replicated, may hold values from 0.05 to 0.3
- gate_logits: bfloat16 [2048, 48], P(('parts', 'ctx', 'pb', 'row')), may hold values from -6 to 6
- chosen_blocks: int32 [32, 16], P(('parts', 'ctx', 'pb', 'row')), may hold values from 0 to 95, as said below
- valid_counts: int32 [32], P(('parts', 'ctx', 'pb', 'row')), may hold values from 4 to 16
Outputs:
- mixed: bfloat16 [2048, 2048], P(('parts', 'ctx', 'pb', 'row'))
Inputs may be any that keep to these rules, and one draw needn't show every extreme that they name: `chosen_blocks`: slot 0 of tile t holds the tile's own block 64 + t. Slot s > 0 holds a block of the cache stored by ctx index (c + s) mod (4), where c is the ctx index that holds tile t; the blocks of one tile are distinct. Slots at or beyond the tile's valid count hold blocks too and are ignored.
All inputs are finite; a program needn't handle non-finite values.
Results may differ from a plain program's by a relative error of at most 0.0034.
The roundings to bfloat16 on the way count: a program that leaves them out, or rounds other values in their place, can miss the bound.
Values may be sent and summed in bfloat16 or wider, within the bound.
A program may use at most 64 MiB of HBM per device.

v0:
```python
import math
import jax
import jax.numpy as jnp
from jax import lax
from jax.sharding import PartitionSpec as P

HEADS = 16
CLEN = 32
STRIDE = 16
BLOCK = 64
WINDOW = 256
NEG_FILL = -1e30


def from_behind(value, axis, steps):
    count = lax.axis_size(axis)
    pairs = [(source, (source + steps) % count) for source in range(count)]
    return lax.ppermute(value, axis, pairs)


def pool_blocks(rows, extra, weights, stride):
    joined = jnp.concatenate([rows, extra], axis=0).astype(jnp.float32)
    blocks = rows.shape[0] // stride
    grouped = joined.reshape(blocks + 1, stride, rows.shape[1])
    leading = jnp.sum(grouped[:-1] * weights[None, :stride, :], axis=1)
    trailing = jnp.sum(grouped[1:] * weights[None, stride:, :], axis=1)
    return (leading + trailing).astype(jnp.bfloat16)


def attend(query_rows, keys, values, visible, score_scale):
    scores = jnp.dot(query_rows, keys.T, preferred_element_type=jnp.float32) * score_scale
    scores = jnp.where(visible, scores, NEG_FILL)
    highest = jnp.max(scores, axis=1, keepdims=True)
    exponent = jnp.where(visible, jnp.exp(scores - highest), 0.0)
    weights = exponent.astype(jnp.bfloat16)
    numerator = jnp.dot(weights, values, preferred_element_type=jnp.float32)
    return numerator / jnp.sum(exponent, axis=1, keepdims=True)


def local(
    queries,
    cache_keys,
    cache_values,
    span_keys,
    span_values,
    pool_keys,
    pool_values,
    gate_logits,
    chosen_blocks,
    valid_counts,
):
    owners = lax.axis_size("ctx")
    ctx_place = lax.axis_index("ctx")
    tile_place = lax.axis_index("pb") * lax.axis_size("row") + lax.axis_index("row")
    cache_len, key_width = cache_keys.shape
    value_width = cache_values.shape[1]
    span_len = span_keys.shape[0]
    tokens = queries.shape[0]
    tiles_here = chosen_blocks.shape[0]
    score_scale = 1.0 / math.sqrt(key_width)
    context_start = cache_len * owners
    local_start = tile_place * tokens
    first_pos = context_start + ctx_place * span_len + local_start
    row_count = tokens * HEADS
    query_rows = queries.reshape(row_count, key_width)
    row_pos = first_pos + jnp.arange(row_count, dtype=jnp.int32) // HEADS
    leader = ctx_place == 0
    outgoing = (
        jnp.where(leader, span_keys[:STRIDE], cache_keys[:STRIDE]),
        jnp.where(leader, span_values[:STRIDE], cache_values[:STRIDE]),
        span_keys[:STRIDE],
        span_values[:STRIDE],
    )
    heads_next = from_behind((outgoing[0], outgoing[1], outgoing[2], outgoing[3]), "ctx", -1)
    summary_keys = jnp.concatenate(
        [
            pool_blocks(cache_keys, heads_next[0], pool_keys, STRIDE),
            pool_blocks(span_keys, heads_next[2], pool_keys, STRIDE),
        ],
        axis=0,
    )
    summary_values = jnp.concatenate(
        [
            pool_blocks(cache_values, heads_next[1], pool_values, STRIDE),
            pool_blocks(span_values, heads_next[3], pool_values, STRIDE),
        ],
        axis=0,
    )
    cache_blocks = cache_len // STRIDE
    span_blocks = span_len // STRIDE
    per_ctx = cache_blocks + span_blocks
    first_row = jnp.int32(0)
    running_max = jnp.full((row_count,), NEG_FILL, jnp.float32)
    running_sum = jnp.zeros((row_count,), jnp.float32)
    running_out = jnp.zeros((row_count, value_width), jnp.float32)
    part_keys = lax.all_gather(summary_keys, "ctx", axis=0, tiled=True)
    part_values = lax.all_gather(summary_values, "ctx", axis=0, tiled=True)
    length = part_keys.shape[0]
    for lower_row in range(0, length, 512):
        upper_row = min(lower_row + 512, length)
        block_index = first_row + lower_row + jnp.arange(upper_row - lower_row, dtype=jnp.int32)
        owner_of = block_index // per_ctx
        within = block_index % per_ctx
        block_id = jnp.where(
            within < cache_blocks,
            owner_of * cache_blocks + within,
            owners * cache_blocks + owner_of * span_blocks + within - cache_blocks,
        )
        visible = (block_id * STRIDE + CLEN)[None, :] <= row_pos[:, None] + 1
        scores = (
            jnp.dot(
                query_rows, part_keys[lower_row:upper_row].T, preferred_element_type=jnp.float32
            )
            * score_scale
        )
        scores = jnp.where(visible, scores, NEG_FILL)
        new_max = jnp.maximum(running_max, jnp.max(scores, axis=1))
        exponent = jnp.where(visible, jnp.exp(scores - new_max[:, None]), 0.0)
        fading = jnp.exp(running_max - new_max)
        running_sum = running_sum * fading + jnp.sum(exponent, axis=1)
        running_out = running_out * fading[:, None] + jnp.dot(
            exponent.astype(jnp.bfloat16),
            part_values[lower_row:upper_row],
            preferred_element_type=jnp.float32,
        )
        running_max = new_max
    summary_out = running_out / running_sum[:, None]
    reach = chosen_blocks.shape[1] // owners
    arranged = chosen_blocks.reshape(tiles_here, reach, owners)
    column_of = (jnp.arange(owners, dtype=jnp.int32) - ctx_place) % owners
    requested = jnp.take(arranged, column_of, axis=2)
    wanted = lax.all_to_all(requested, "ctx", split_axis=2, concat_axis=2, tiled=True)
    cache_count = cache_len // BLOCK
    span_count = span_len // BLOCK
    from_cache = (wanted < owners * cache_count)[..., None, None]
    cache_slot = jnp.clip(wanted - ctx_place * cache_count, 0, cache_count - 1)
    span_slot = jnp.clip(wanted - owners * cache_count - ctx_place * span_count, 0, span_count - 1)
    served_keys = jnp.where(
        from_cache,
        cache_keys.reshape(cache_count, BLOCK, key_width)[cache_slot],
        span_keys.reshape(span_count, BLOCK, key_width)[span_slot],
    )
    served_values = jnp.where(
        from_cache,
        cache_values.reshape(cache_count, BLOCK, value_width)[cache_slot],
        span_values.reshape(span_count, BLOCK, value_width)[span_slot],
    )
    fetched_keys, fetched_values = (
        lax.all_to_all(served_keys, "ctx", split_axis=2, concat_axis=2, tiled=True),
        lax.all_to_all(served_values, "ctx", split_axis=2, concat_axis=2, tiled=True),
    )
    last_ctx = ctx_place == owners - 1
    tail_rows = from_behind(
        (
            jnp.where(last_ctx, cache_keys[-WINDOW:], span_keys[-WINDOW:]),
            jnp.where(last_ctx, cache_values[-WINDOW:], span_values[-WINDOW:]),
        ),
        "ctx",
        1,
    )
    reach_keys = jnp.concatenate([tail_rows[0], span_keys], axis=0)
    reach_values = jnp.concatenate([tail_rows[1], span_values], axis=0)
    gate_values = jax.nn.sigmoid(gate_logits.astype(jnp.float32)).reshape(tokens, 3, HEADS)
    offsets = jnp.arange(BLOCK, dtype=jnp.int32)
    near_offsets = jnp.arange(WINDOW + BLOCK, dtype=jnp.int32)
    slot_number = jnp.arange(reach, dtype=jnp.int32)[:, None] * owners + column_of[None, :]
    key_pos = (requested[0][:, :, None] * BLOCK + offsets).reshape(-1)
    usable = jnp.repeat((slot_number < valid_counts[0]).reshape(-1), BLOCK)
    sel_visible = usable[None, :] & (key_pos[None, :] <= row_pos[:, None])
    picked = attend(
        query_rows,
        fetched_keys[0].reshape(-1, key_width),
        fetched_values[0].reshape(-1, value_width),
        sel_visible,
        score_scale,
    )
    begin = local_start + 0
    near_keys = lax.dynamic_slice_in_dim(reach_keys, begin, WINDOW + BLOCK, 0)
    near_values = lax.dynamic_slice_in_dim(reach_values, begin, WINDOW + BLOCK, 0)
    near_pos = context_start + ctx_place * span_len - WINDOW + begin + near_offsets
    near_visible = (near_pos[None, :] <= row_pos[:, None]) & (
        near_pos[None, :] > row_pos[:, None] - WINDOW
    )
    nearby = attend(query_rows, near_keys, near_values, near_visible, score_scale)
    mixed = (
        gate_values[:, 0, :, None] * summary_out.reshape(BLOCK, HEADS, value_width)
        + gate_values[:, 1, :, None] * picked.reshape(BLOCK, HEADS, value_width)
        + gate_values[:, 2, :, None] * nearby.reshape(BLOCK, HEADS, value_width)
    )
    outputs = mixed.reshape(BLOCK, HEADS * value_width).astype(jnp.bfloat16)
    return outputs


def solution(mesh):
    return jax.shard_map(
        local,
        mesh=mesh,
        in_specs=(
            P(("parts", "ctx", "pb", "row"), None),
            P(("parts", "ctx"), None),
            P(("parts", "ctx"), None),
            P(("parts", "ctx"), None),
            P(("parts", "ctx"), None),
            P(),
            P(),
            P(("parts", "ctx", "pb", "row"), None),
            P(("parts", "ctx", "pb", "row"), None),
            P(("parts", "ctx", "pb", "row")),
        ),
        out_specs=P(("parts", "ctx", "pb", "row"), None),
        check_vma=False,
    )
```

profile of v0, /device:TPU:0, one launch (start us, length us, event | category | flops | bytes accessed | tf_op | source)
XLA Modules:
  0.0 91.8 jit_solution(5316688061465802636)
XLA Ops:
  0.0 1.3 %copy.79 = bf16[1024,192]{1,0:T(8,128)(2,1)S(1)} copy(bf16[1024,192]{0,1:T(8,128)(2,1)} %param.11) | data formatting | bytes 786432 | tf_op args[1]
  1.3 1.1 %copy.77 = bf16[512,192]{1,0:T(8,128)(2,1)S(1)} copy(bf16[512,192]{0,1:T(8,128)(2,1)} %param.13) | data formatting | bytes 393216 | tf_op args[3]
  3.0 5.1 %collective-permute-start = (bf16[16,192]{1,0:T(8,128)(2,1)}, bf16[16,192]{1,0:T(8,128)(2,1)}, u32[]{:S(2)}, u32[]{:S(2)}) collective-permute-start(bf16[16,192]{1,0:T(8,128)(2,1)} %get-tuple-element.13), channel_id=1, source_target_pairs={{0,24},{8,0},{16,8},{24,16},{1,25},{9,1},{17,9},{25,17},{2,26},{10... | collective-permute-start | bytes 18440 | tf_op jit(solution)/shard_map/ppermute | solution.py:18
  8.5 1.3 %slice_select_fusion.3 = (bf16[16,128]{1,0:T(8,128)(2,1)}, bf16[16,128]{1,0:T(8,128)(2,1)}) fusion(bf16[1024,128]{1,0:T(8,128)(2,1)} %param.12, pred[]{:T(512)S(6)} %eq.10, bf16[512,128]{1,0:T(8,128)(2,1)} %param.14), kind=kLoop, calls=%fused_computation.87 | loop fusion | flops 2048 | bytes 16385 | tf_op jit(solution)/shard_map/jit(_where)/select_n | solution.py:70
  10.8 1.3 %reduce.3 = s32[16]{0:T(128)S(1)} reduce(s32[1,16]{1,0:T(1,128)} %param.18, s32[]{:T(128)} %broadcast.494), dimensions={0}, to_apply=%param.18.reduce_sub_computation.3 | reduce | bytes 132 | tf_op args[8]
  13.7 5.3 %all-to-all-start = ((s32[1,4,4]{1,0,2:T(1,128)}), s32[1,4,4]{1,0,2:T(1,128)S(1)}, u32[]{:S(2)}, u32[]{:S(2)}) async-start(s32[1,4,4]{1,0,2:T(1,128)} %copy.85), calls=%async_computation | async-start | bytes 4096 | tf_op jit(solution)/shard_map/all_to_all | solution.py:132
  18.9 1.0 %slice_select_fusion = bf16[256,192]{0,1:T(8,128)(2,1)S(1)} fusion(bf16[512,192]{0,1:T(8,128)(2,1)} %param.13, bf16[1024,192]{0,1:T(8,128)(2,1)} %param.11, pred[]{:T(512)S(6)} %eq.11), kind=kLoop, calls=%fused_computation.60 | loop fusion | flops 49152 | bytes 294913 | tf_op jit(solution)/shard_map/jit(_where)/select_n | solution.py:155
  19.9 2.1 %collective-permute-start.4 = (bf16[256,192]{0,1:T(8,128)(2,1)S(1)}, bf16[256,192]{0,1:T(8,128)(2,1)}, u32[]{:S(2)}, u32[]{:S(2)}) collective-permute-start(bf16[256,192]{0,1:T(8,128)(2,1)S(1)} %slice_select_fusion), channel_id=1, source_target_pairs={{0,8},{8,16},{16,24},{24,0},{1,9},{9,17},{17,25},{25,1},{2,10},{10... | collective-permute-start | bytes 294920 | tf_op jit(solution)/shard_map/ppermute | solution.py:18
  30.3 0.7 copy.95
  31.1 3.6 %all-to-all-start.2 = ((bf16[1,4,4,64,128]{4,3,1,0,2:T(8,128)(2,1)}), bf16[1,4,4,64,128]{4,3,1,0,2:T(8,128)(2,1)S(1)}, u32[]{:S(2)}, u32[]{:S(2)}) async-start(bf16[1,4,4,64,128]{4,3,1,0,2:T(8,128)(2,1)} %copy.95), calls=%async_computation.2 | async-start | bytes 524288 | tf_op jit(solution)/shard_map/all_to_all | solution.py:150
  34.7 0.9 copy_select_fusion
  35.6 2.0 %collective-permute-start.5 = (bf16[256,128]{1,0:T(8,128)(2,1)S(1)}, bf16[256,128]{1,0:T(8,128)(2,1)}, u32[]{:S(2)}, u32[]{:S(2)}) collective-permute-start(bf16[256,128]{1,0:T(8,128)(2,1)S(1)} %slice_select_fusion.1), channel_id=1, source_target_pairs={{0,8},{8,16},{16,24},{24,0},{1,9},{9,17},{17,25},{25,1},{2,10},{10... | collective-permute-start | bytes 196616 | tf_op jit(solution)/shard_map/ppermute | solution.py:18
  39.6 13.2 %all_gather.7 = bf16[384,128]{1,0:T(8,128)(2,1)S(1)} all-gather(bf16[96,128]{1,0:T(8,128)(2,1)S(1)} %pad_maximum_fusion.1), channel_id=1, replica_groups=mesh['parts'=1,'ctx'=4,'pb'=4,'row'=2] {'ctx'}, dimensions={0}, use_global_device_ids=true | all-gather | bytes 122880 | tf_op jit(solution)/shard_map/all_gather | solution.py:97
  52.8 0.8 maximum_convert_fusion
  53.8 0.7 maximum_convert_fusion.1
  55.5 13.6 %all_gather.6 = bf16[384,192]{1,0:T(8,128)(2,1)S(1)} all-gather(bf16[96,192]{1,0:T(8,128)(2,1)S(1)} %pad_maximum_fusion), channel_id=1, replica_groups=mesh['parts'=1,'ctx'=4,'pb'=4,'row'=2] {'ctx'}, dimensions={0}, use_global_device_ids=true | all-gather | bytes 184320 | tf_op jit(solution)/shard_map/all_gather | solution.py:96
  70.6 3.7 %all-to-all-start.1 = ((bf16[1,4,4,64,192]{4,3,1,0,2:T(8,128)(2,1)}), bf16[1,4,4,64,192]{4,3,1,0,2:T(8,128)(2,1)S(1)}, u32[]{:S(2)}, u32[]{:S(2)}) async-start(bf16[1,4,4,64,192]{4,3,1,0,2:T(8,128)(2,1)} %copy_select_fusion), calls=%async_computation.1 | async-start | bytes 1048576 | tf_op jit(solution)/shard_map/all_to_all | solution.py:149
  74.3 1.7 %fusion.59 = (f32[1024]{0:T(1024)S(1)}, f32[1024,320]{0,1:T(8,128)S(1)}) fusion(bf16[1024,192]{1,0:T(8,128)(2,1)S(1)} %reshape.297, s32[]{:T(128)S(6)} %select_n.211, bf16[256,192]{0,1:T(8,128)(2,1)} %collective-permute-done.4, bf16[512,192]{0,1:T(8,128)(2,1)S(1)} %copy-done.2, s32[1024]{0:T(1024)S(1)} %broadcast_add_fusion, s32[1024]{0:T(1024)S(1)} %fusion.31, ...), kind=kOutput, calls=%fused_computation.137 | convolution fusion | flops 128039936 | bytes 2012420 | tf_op jit(solution)/shard_map/dot_general | solution.py:31
  76.4 1.5 %convolution_divide_fusion = f32[1024,128]{1,0:T(8,128)S(1)} fusion(f32[1024,320]{0,1:T(8,128)S(1)} %get-tuple-element.29, f32[1024]{0:T(1024)S(1)} %get-tuple-element.28, s32[1024]{0:T(1024)S(1)} %broadcast_add_fusion, s32[1024]{0:T(1024)S(1)} %fusion.31, s32[320]{0:T(512)S(1)} %iota_add_fusion.1, f32[1024]{0:T(1024)S(1)} %fusion.11, s32[]{:T(128)S(6)} %select_n.211, ...), kind=kOutput, calls=%fused_computation.21 | convolution fusion | flops 86147072 | bytes 2049284 | tf_op jit(solution)/shard_map/dot_general | solution.py:36
  78.0 6.4 %all-to-all-done.1 = bf16[1,4,4,64,192]{4,3,1,0,2:T(8,128)(2,1)S(1)} async-done(((bf16[1,4,4,64,192]{4,3,1,0,2:T(8,128)(2,1)}), bf16[1,4,4,64,192]{4,3,1,0,2:T(8,128)(2,1)S(1)}, u32[]{:S(2)}, u32[]{:S(2)}) %all-to-all-start.1) | async-done | bytes 393248 | tf_op jit(solution)/shard_map/all_to_all | solution.py:149
  84.4 1.2 %fusion = (f32[1024]{0:T(1024)S(1)}, f32[1024,1024]{1,0:T(8,128)S(1)}) fusion(s32[1024]{0:T(1024)S(1)} %fusion.31, s32[1024]{0:T(1024)S(1)} %add.265, pred[1024]{0:T(1024)(128)(4,1)S(1)} %copy-done.11, bf16[1024,192]{1,0:T(8,128)(2,1)S(1)} %bitcast.97, bf16[1024,192]{1,0:T(8,128)(2,1)S(1)} %reshape.297), kind=kOutput, calls=%fused_computation.8 | convolution fusion | flops 407895040 | bytes 4994048 | tf_op jit(solution)/shard_map/dot_general | solution.py:31
  85.6 1.9 %fusion.52 = f32[1024]{0:T(1024)S(1)} fusion(f32[1024]{0:T(1024)S(1)} %get-tuple-element.30, f32[1024,1024]{1,0:T(8,128)S(1)} %get-tuple-element.31, s32[1024]{0:T(1024)S(1)} %fusion.31, s32[1024]{0:T(1024)S(1)} %add.265, pred[1024]{0:T(1024)(128)(4,1)S(1)} %copy-done.11), kind=kLoop, calls=%fused_computation.130 | loop fusion | flops 7339008 | bytes 4211712 | tf_op jit(solution)/shard_map/reduce_sum | solution.py:37
  87.5 1.8 %fusion.6 = f32[1024,128]{1,0:T(8,128)S(1)} fusion(bf16[1024,128]{1,0:T(8,128)(2,1)S(1)} %bitcast.98, f32[1024]{0:T(1024)S(1)} %fusion.52, f32[1024,1024]{1,0:T(8,128)S(1)} %get-tuple-element.31, f32[1024]{0:T(1024)S(1)} %get-tuple-element.30, s32[1024]{0:T(1024)S(1)} %fusion.31, s32[1024]{0:T(1024)S(1)} %add.265, pred[1024]{0:T(1024)(128)(4,1)S(1)} %copy-done.11), kind=kOutput, calls=%fused_computation.20 | convolution fusion | flops 275906560 | bytes 4998144 | tf_op jit(solution)/shard_map/dot_general | solution.py:36
  90.6 1.3 %fusion.25 = bf16[64,2048]{1,0:T(8,128)(2,1)} fusion(f32[64,2048]{1,0:T(8,128)S(1)} %reshape.305, f32[8,8,16,128]{3,2,1,0:T(8,128)S(1)} %bitcast.92, f32[64,2048]{1,0:T(8,128)S(1)} %reshape.304, f32[8,8,16,128]{3,2,1,0:T(8,128)S(1)} %bitcast.91, f32[64,2048]{1,0:T(8,128)S(1)} %reshape.298, f32[8,8,16,128]{3,2,1,0:T(8,128)S(1)} %bitcast.90), kind=kLoop, calls=%fused_computation.40 | loop fusion | flops 786432 | bytes 3407872 | tf_op jit(solution)/shard_map/convert_element_type | solution.py:190
  (115 shorter events, 17.3 us)
Async XLA Ops:
  0.0 22.7 %copy-start.1 = (bf16[1024,128]{1,0:T(8,128)(2,1)S(1)}, bf16[1024,128]{1,0:T(8,128)(2,1)}, u32[]{:S(2)}) copy-start(bf16[1024,128]{1,0:T(8,128)(2,1)} %param.12) | copy-start | bytes 786436
  0.0 22.7 %copy-start = (bf16[512,128]{1,0:T(8,128)(2,1)S(1)}, bf16[512,128]{1,0:T(8,128)(2,1)}, u32[]{:S(2)}) copy-start(bf16[512,128]{1,0:T(8,128)(2,1)} %param.14) | copy-start | bytes 393220
  0.0 22.7 %copy-start.7 = (f32[32,192]{1,0:T(8,128)S(1)}, f32[32,192]{1,0:T(8,128)}, u32[]{:S(2)}) copy-start(f32[32,192]{1,0:T(8,128)} %param.15) | copy-start | bytes 73732
  0.0 22.7 %copy-start.3 = (bf16[64,3072]{1,0:T(8,128)(2,1)S(1)}, bf16[64,3072]{1,0:T(8,128)(2,1)}, u32[]{:S(2)}) copy-start(bf16[64,3072]{1,0:T(8,128)(2,1)} %param.10) | copy-start | bytes 1179652
  0.0 23.4 %copy-start.8 = (f32[32,128]{1,0:T(8,128)S(1)}, f32[32,128]{1,0:T(8,128)}, u32[]{:S(2)}) copy-start(f32[32,128]{1,0:T(8,128)} %param.16) | copy-start | bytes 49156
  0.0 25.2 %copy-start.9 = (bf16[64,48]{0,1:T(8,128)(2,1)S(1)}, bf16[64,48]{0,1:T(8,128)(2,1)}, u32[]{:S(2)}) copy-start(bf16[64,48]{0,1:T(8,128)(2,1)} %param.17) | copy-start | bytes 18436
  3.0 49.8 %collective-permute-start = (bf16[16,192]{1,0:T(8,128)(2,1)}, bf16[16,192]{1,0:T(8,128)(2,1)}, u32[]{:S(2)}, u32[]{:S(2)}) collective-permute-start(bf16[16,192]{1,0:T(8,128)(2,1)} %get-tuple-element.13), channel_id=1, source_target_pairs={{0,24},{8,0},{16,8},{24,16},{1,25},{9,1},{17,9},{25,17},{2,26},{10... | collective-permute-start | bytes 18440 | tf_op jit(solution)/shard_map/ppermute | solution.py:18
  8.0 45.7 %collective-permute-start.1 = (bf16[16,192]{1,0:T(8,128)(2,1)}, bf16[16,192]{1,0:T(8,128)(2,1)}, u32[]{:S(2)}, u32[]{:S(2)}) collective-permute-start(bf16[16,192]{1,0:T(8,128)(2,1)} %get-tuple-element.14), channel_id=1, source_target_pairs={{0,24},{8,0},{16,8},{24,16},{1,25},{9,1},{17,9},{25,17},{2,26},{10... | collective-permute-start | bytes 18440 | tf_op jit(solution)/shard_map/ppermute | solution.py:18
  9.8 25.8 %collective-permute-start.2 = (bf16[16,128]{1,0:T(8,128)(2,1)}, bf16[16,128]{1,0:T(8,128)(2,1)}, u32[]{:S(2)}, u32[]{:S(2)}) collective-permute-start(bf16[16,128]{1,0:T(8,128)(2,1)} %get-tuple-element.15), channel_id=1, source_target_pairs={{0,24},{8,0},{16,8},{24,16},{1,25},{9,1},{17,9},{25,17},{2,26},{10... | collective-permute-start | bytes 12296 | tf_op jit(solution)/shard_map/ppermute | solution.py:18
  10.2 28.2 %collective-permute-start.3 = (bf16[16,128]{1,0:T(8,128)(2,1)}, bf16[16,128]{1,0:T(8,128)(2,1)}, u32[]{:S(2)}, u32[]{:S(2)}) collective-permute-start(bf16[16,128]{1,0:T(8,128)(2,1)} %get-tuple-element.16), channel_id=1, source_target_pairs={{0,24},{8,0},{16,8},{24,16},{1,25},{9,1},{17,9},{25,17},{2,26},{10... | collective-permute-start | bytes 12296 | tf_op jit(solution)/shard_map/ppermute | solution.py:18
  13.7 13.6 %all-to-all-start = ((s32[1,4,4]{1,0,2:T(1,128)}), s32[1,4,4]{1,0,2:T(1,128)S(1)}, u32[]{:S(2)}, u32[]{:S(2)}) async-start(s32[1,4,4]{1,0,2:T(1,128)} %copy.85), calls=%async_computation | async-start | bytes 4096 | tf_op jit(solution)/shard_map/all_to_all | solution.py:132
  19.9 54.4 %collective-permute-start.4 = (bf16[256,192]{0,1:T(8,128)(2,1)S(1)}, bf16[256,192]{0,1:T(8,128)(2,1)}, u32[]{:S(2)}, u32[]{:S(2)}) collective-permute-start(bf16[256,192]{0,1:T(8,128)(2,1)S(1)} %slice_select_fusion), channel_id=1, source_target_pairs={{0,8},{8,16},{16,24},{24,0},{1,9},{9,17},{17,25},{25,1},{2,10},{10... | collective-permute-start | bytes 294920 | tf_op jit(solution)/shard_map/ppermute | solution.py:18
  31.1 39.6 %all-to-all-start.2 = ((bf16[1,4,4,64,128]{4,3,1,0,2:T(8,128)(2,1)}), bf16[1,4,4,64,128]{4,3,1,0,2:T(8,128)(2,1)S(1)}, u32[]{:S(2)}, u32[]{:S(2)}) async-start(bf16[1,4,4,64,128]{4,3,1,0,2:T(8,128)(2,1)} %copy.95), calls=%async_computation.2 | async-start | bytes 524288 | tf_op jit(solution)/shard_map/all_to_all | solution.py:150
  35.6 40.8 %collective-permute-start.5 = (bf16[256,128]{1,0:T(8,128)(2,1)S(1)}, bf16[256,128]{1,0:T(8,128)(2,1)}, u32[]{:S(2)}, u32[]{:S(2)}) collective-permute-start(bf16[256,128]{1,0:T(8,128)(2,1)S(1)} %slice_select_fusion.1), channel_id=1, source_target_pairs={{0,8},{8,16},{16,24},{24,0},{1,9},{9,17},{17,25},{25,1},{2,10},{10... | collective-permute-start | bytes 196616 | tf_op jit(solution)/shard_map/ppermute | solution.py:18
  54.6 14.4 %copy-start.10 = (s32[384]{0:T(512)S(1)}, s32[384]{0:T(512)}, u32[]{:S(2)}) copy-start(s32[384]{0:T(512)} %multiply_add_fusion) | copy-start | bytes 4612
  70.5 3.8 %copy-start.2 = (bf16[512,192]{0,1:T(8,128)(2,1)S(1)}, bf16[512,192]{0,1:T(8,128)(2,1)}, u32[]{:S(2)}) copy-start(bf16[512,192]{0,1:T(8,128)(2,1)} %param.13) | copy-start | bytes 589828
  70.6 13.7 %all-to-all-start.1 = ((bf16[1,4,4,64,192]{4,3,1,0,2:T(8,128)(2,1)}), bf16[1,4,4,64,192]{4,3,1,0,2:T(8,128)(2,1)S(1)}, u32[]{:S(2)}, u32[]{:S(2)}) async-start(bf16[1,4,4,64,192]{4,3,1,0,2:T(8,128)(2,1)} %copy_select_fusion), calls=%async_computation.1 | async-start | bytes 1048576 | tf_op jit(solution)/shard_map/all_to_all | solution.py:149
  77.9 6.5 %copy-start.11 = (pred[1024]{0:T(1024)(128)(4,1)S(1)}, pred[1024]{0:T(1024)(128)(4,1)}, u32[]{:S(2)}) copy-start(pred[1024]{0:T(1024)(128)(4,1)} %and.99) | copy-start | bytes 3076
  87.5 2.0 %copy-start.4 = (f32[64,16]{1,0:T(8,128)S(1)}, f32[64,16]{1,0:T(8,128)}, u32[]{:S(2)}) copy-start(f32[64,16]{1,0:T(8,128)} %copy.76) | copy-start | bytes 12292
  89.4 0.8 copy-start.5
  89.4 0.9 %copy-start.6 = (f32[64,16]{1,0:T(8,128)S(1)}, f32[64,16]{1,0:T(8,128)}, u32[]{:S(2)}) copy-start(f32[64,16]{1,0:T(8,128)} %copy.97) | copy-start | bytes 12292
where the time goes:
time: 92.6 us; the launch traced here: 91.8 us
  blocking collectives  26.8 us (29%)
  starting transfers between devices  22.7 us (25%)
  other arithmetic  14.1 us (15%)
  local copies, waits for them, and re-layouts  13.3 us (14%)
  matrix products  7.31 us (8%)
  waiting for transfers between devices  6.38 us (7%)
  between operations  1.25 us (1%)
    all_gather x1, blocking collectives, local(): part_keys = lax.all_gather(summary_keys, 'ctx', axis=0, tiled=True)  13.6 us
    all_gather x1, blocking collectives, local(): part_values = lax.all_gather(summary_values, 'ctx', axis=0, tiled=True)  13.2 us
    ppermute x6, starting transfers between devices, from_behind(): return lax.ppermute(value, axis, pairs)  10.1 us
    all_to_all x1, waiting for transfers between devices, local(): lax.all_to_all(served_keys, 'ctx', split_axis=2, concat_axis=2, tiled=True)  6.36 us
    all_to_all x1, starting transfers between devices, local(): lax.all_to_all(requested, 'ctx', split_axis=2, concat_axis=2, tiled=True)  5.27 us
    all_to_all x1, starting transfers between devices, local(): lax.all_to_all(served_keys, 'ctx', split_axis=2, concat_axis=2, tiled=True)  3.66 us
    all_to_all x1, starting transfers between devices, local(): lax.all_to_all(served_values, 'ctx', split_axis=2, concat_axis=2, tiled=T...  3.63 us
    unnamed x27, local copies, waits for them, and re-layouts  3.33 us
  transfers between devices with their start and end apart: 9, of which 1 were waited for; matrix products, arithmetic and copies ran while one was open for 27% of the time, Pallas kernels for 0%

commit v1 on v0

--- a/solution.py
+++ b/solution.py
@@ -93,8 +93,9 @@
     running_max = jnp.full((row_count,), NEG_FILL, jnp.float32)
     running_sum = jnp.zeros((row_count,), jnp.float32)
     running_out = jnp.zeros((row_count, value_width), jnp.float32)
-    part_keys = lax.all_gather(summary_keys, "ctx", axis=0, tiled=True)
-    part_values = lax.all_gather(summary_values, "ctx", axis=0, tiled=True)
+    val2 = jnp.concatenate([summary_keys, summary_values], 1)
+    built = lax.all_gather(val2, "ctx", axis=0, tiled=True)
+    part_keys, part_values = jnp.split(built, [summary_keys.shape[1]], 1)
     length = part_keys.shape[0]
     for lower_row in range(0, length, 512):
         upper_row = min(lower_row + 512, length)

time: 92.6 us -> 79.8 us (0.86)
  blocking collectives: 26.8 us -> 13.9 us
    all_gather x2 -> x1, blocking collectives: 26.8 us -> 13.9 us  [local(): built = lax.all_gather(val2, 'ctx', axis=0, tiled=True)]
  transfers between devices with their start and end apart: 9 -> 9, of which waited for: 1 -> 1; matrix products, arithmetic and copies ran while one was open for 27% -> 31% of each run, Pallas kernels for 0% -> 0%
where the time goes in v1:
time: 79.8 us; the launch traced here: 79.1 us
  starting transfers between devices  22.7 us (28%)
  other arithmetic  14.2 us (18%)
  blocking collectives  13.9 us (17%)
  local copies, waits for them, and re-layouts  13.3 us (17%)
  matrix products  7.39 us (9%)
  waiting for transfers between devices  6.38 us (8%)
  between operations  1.24 us (2%)
    all_gather x1, blocking collectives, local(): built = lax.all_gather(val2, 'ctx', axis=0, tiled=True)  13.9 us
    ppermute x6, starting transfers between devices, from_behind(): return lax.ppermute(value, axis, pairs)  10.1 us
    all_to_all x1, waiting for transfers between devices, local(): lax.all_to_all(served_keys, 'ctx', split_axis=2, concat_axis=2, tiled=True)  6.36 us
    all_to_all x1, starting transfers between devices, local(): lax.all_to_all(requested, 'ctx', split_axis=2, concat_axis=2, tiled=True)  5.27 us
    all_to_all x1, starting transfers between devices, local(): lax.all_to_all(served_keys, 'ctx', split_axis=2, concat_axis=2, tiled=True)  3.66 us
    all_to_all x1, starting transfers between devices, local(): lax.all_to_all(served_values, 'ctx', split_axis=2, concat_axis=2, tiled=T...  3.63 us
    unnamed x27, local copies, waits for them, and re-layouts  3.33 us
    dot_general x2, matrix products, attend(): numerator = jnp.dot(weights, values, preferred_element_type=jnp.float32)  3.33 us
  transfers between devices with their start and end apart: 9, of which 1 were waited for; matrix products, arithmetic and copies ran while one was open for 31% of the time, Pallas kernels for 0%

profile of v1, /device:TPU:0, one launch (start us, length us, event | category | flops | bytes accessed | tf_op | source)
XLA Modules:
  0.0 79.1 jit_solution(2158337222110354219)
XLA Ops:
  0.0 1.3 %copy.79 = bf16[1024,192]{1,0:T(8,128)(2,1)S(1)} copy(bf16[1024,192]{0,1:T(8,128)(2,1)} %param.11) | data formatting | bytes 786432 | tf_op args[1]
  1.3 1.1 %copy.77 = bf16[512,192]{1,0:T(8,128)(2,1)S(1)} copy(bf16[512,192]{0,1:T(8,128)(2,1)} %param.13) | data formatting | bytes 393216 | tf_op args[3]
  3.0 5.1 %collective-permute-start = (bf16[16,192]{1,0:T(8,128)(2,1)}, bf16[16,192]{1,0:T(8,128)(2,1)}, u32[]{:S(2)}, u32[]{:S(2)}) collective-permute-start(bf16[16,192]{1,0:T(8,128)(2,1)} %get-tuple-element.13), channel_id=1, source_target_pairs={{0,24},{8,0},{16,8},{24,16},{1,25},{9,1},{17,9},{25,17},{2,26},{10... | collective-permute-start | bytes 18440 | tf_op jit(solution)/shard_map/ppermute | solution.py:18
  8.5 1.3 %slice_select_fusion.3 = (bf16[16,128]{1,0:T(8,128)(2,1)}, bf16[16,128]{1,0:T(8,128)(2,1)}) fusion(bf16[1024,128]{1,0:T(8,128)(2,1)} %param.12, pred[]{:T(512)S(6)} %eq.10, bf16[512,128]{1,0:T(8,128)(2,1)} %param.14), kind=kLoop, calls=%fused_computation.89 | loop fusion | flops 2048 | bytes 16385 | tf_op jit(solution)/shard_map/jit(_where)/select_n | solution.py:70
  10.8 1.3 %reduce.3 = s32[16]{0:T(128)S(1)} reduce(s32[1,16]{1,0:T(1,128)} %param.18, s32[]{:T(128)} %broadcast.494), dimensions={0}, to_apply=%param.18.reduce_sub_computation.3 | reduce | bytes 132 | tf_op args[8]
  13.7 5.3 %all-to-all-start = ((s32[1,4,4]{1,0,2:T(1,128)}), s32[1,4,4]{1,0,2:T(1,128)S(1)}, u32[]{:S(2)}, u32[]{:S(2)}) async-start(s32[1,4,4]{1,0,2:T(1,128)} %copy.85), calls=%async_computation | async-start | bytes 4096 | tf_op jit(solution)/shard_map/all_to_all | solution.py:133
  18.9 1.0 %slice_select_fusion = bf16[256,192]{0,1:T(8,128)(2,1)S(1)} fusion(bf16[512,192]{0,1:T(8,128)(2,1)} %param.13, bf16[1024,192]{0,1:T(8,128)(2,1)} %param.11, pred[]{:T(512)S(6)} %eq.11), kind=kLoop, calls=%fused_computation.62 | loop fusion | flops 49152 | bytes 294913 | tf_op jit(solution)/shard_map/jit(_where)/select_n | solution.py:156
  19.9 2.1 %collective-permute-start.4 = (bf16[256,192]{0,1:T(8,128)(2,1)S(1)}, bf16[256,192]{0,1:T(8,128)(2,1)}, u32[]{:S(2)}, u32[]{:S(2)}) collective-permute-start(bf16[256,192]{0,1:T(8,128)(2,1)S(1)} %slice_select_fusion), channel_id=1, source_target_pairs={{0,8},{8,16},{16,24},{24,0},{1,9},{9,17},{17,25},{25,1},{2,10},{10... | collective-permute-start | bytes 294920 | tf_op jit(solution)/shard_map/ppermute | solution.py:18
  30.4 0.7 copy.95
  31.1 3.6 %all-to-all-start.2 = ((bf16[1,4,4,64,128]{4,3,1,0,2:T(8,128)(2,1)}), bf16[1,4,4,64,128]{4,3,1,0,2:T(8,128)(2,1)S(1)}, u32[]{:S(2)}, u32[]{:S(2)}) async-start(bf16[1,4,4,64,128]{4,3,1,0,2:T(8,128)(2,1)} %copy.95), calls=%async_computation.2 | async-start | bytes 524288 | tf_op jit(solution)/shard_map/all_to_all | solution.py:151
  34.7 0.9 %copy_select_fusion = bf16[1,4,4,64,192]{4,3,1,0,2:T(8,128)(2,1)} fusion(bf16[1,4,4,64,192]{4,3,2,1,0:T(8,128)(2,1)S(1)} %bitcast.87, bf16[1,4,4,64,192]{4,3,2,1,0:T(8,128)(2,1)S(1)} %bitcast.86, pred[4,4]{0,1:T(4,128)(4,1)S(1)} %copy.87), kind=kLoop, calls=%fused_computation.44 | loop fusion | flops 196608 | bytes 1179664 | tf_op jit(solution)/shard_map/jit(_where)/select_n | solution.py:139
  35.6 2.0 %collective-permute-start.5 = (bf16[256,128]{1,0:T(8,128)(2,1)S(1)}, bf16[256,128]{1,0:T(8,128)(2,1)}, u32[]{:S(2)}, u32[]{:S(2)}) collective-permute-start(bf16[256,128]{1,0:T(8,128)(2,1)S(1)} %slice_select_fusion.1), channel_id=1, source_target_pairs={{0,8},{8,16},{16,24},{24,0},{1,9},{9,17},{17,25},{25,1},{2,10},{10... | collective-permute-start | bytes 196616 | tf_op jit(solution)/shard_map/ppermute | solution.py:18
  39.6 0.8 maximum_convert_fusion
  40.5 0.7 maximum_convert_fusion.1
  42.3 13.9 %all_gather.3 = bf16[384,320]{1,0:T(8,128)(2,1)S(1)} all-gather(bf16[96,320]{1,0:T(8,128)(2,1)S(1)} %maximum_maximum_fusion), channel_id=1, replica_groups=mesh['parts'=1,'ctx'=4,'pb'=4,'row'=2] {'ctx'}, dimensions={0}, use_global_device_ids=true | all-gather | bytes 307200 | tf_op jit(solution)/shard_map/all_gather | solution.py:97
  57.0 0.8 fusion.5
  57.9 3.7 %all-to-all-start.1 = ((bf16[1,4,4,64,192]{4,3,1,0,2:T(8,128)(2,1)}), bf16[1,4,4,64,192]{4,3,1,0,2:T(8,128)(2,1)S(1)}, u32[]{:S(2)}, u32[]{:S(2)}) async-start(bf16[1,4,4,64,192]{4,3,1,0,2:T(8,128)(2,1)} %copy_select_fusion), calls=%async_computation.1 | async-start | bytes 1048576 | tf_op jit(solution)/shard_map/all_to_all | solution.py:150
  61.6 1.7 %fusion.61 = (f32[1024]{0:T(1024)S(1)}, f32[1024,320]{0,1:T(8,128)S(1)}) fusion(bf16[1024,192]{1,0:T(8,128)(2,1)S(1)} %reshape.297, s32[]{:T(128)S(6)} %select_n.211, bf16[256,192]{0,1:T(8,128)(2,1)} %collective-permute-done.4, bf16[512,192]{0,1:T(8,128)(2,1)S(1)} %copy-done.2, s32[1024]{0:T(1024)S(1)} %broadcast_add_fusion, s32[1024]{0:T(1024)S(1)} %fusion.33, ...), kind=kOutput, calls=%fused_computation.138 | convolution fusion | flops 128039936 | bytes 2012420 | tf_op jit(solution)/shard_map/dot_general | solution.py:31
  63.6 1.5 %convolution_divide_fusion = f32[1024,128]{1,0:T(8,128)S(1)} fusion(f32[1024,320]{0,1:T(8,128)S(1)} %get-tuple-element.29, f32[1024]{0:T(1024)S(1)} %get-tuple-element.28, s32[1024]{0:T(1024)S(1)} %broadcast_add_fusion, s32[1024]{0:T(1024)S(1)} %fusion.33, s32[320]{0:T(512)S(1)} %iota_add_fusion.1, f32[1024]{0:T(1024)S(1)} %fusion.11, s32[]{:T(128)S(6)} %select_n.211, ...), kind=kOutput, calls=%fused_computation.21 | convolution fusion | flops 86147072 | bytes 2049284 | tf_op jit(solution)/shard_map/dot_general | solution.py:36
  65.3 6.4 %all-to-all-done.1 = bf16[1,4,4,64,192]{4,3,1,0,2:T(8,128)(2,1)S(1)} async-done(((bf16[1,4,4,64,192]{4,3,1,0,2:T(8,128)(2,1)}), bf16[1,4,4,64,192]{4,3,1,0,2:T(8,128)(2,1)S(1)}, u32[]{:S(2)}, u32[]{:S(2)}) %all-to-all-start.1) | async-done | bytes 393248 | tf_op jit(solution)/shard_map/all_to_all | solution.py:150
  71.7 1.2 %fusion = (f32[1024]{0:T(1024)S(1)}, f32[1024,1024]{1,0:T(8,128)S(1)}) fusion(s32[1024]{0:T(1024)S(1)} %fusion.33, s32[1024]{0:T(1024)S(1)} %add.265, pred[1024]{0:T(1024)(128)(4,1)S(1)} %copy-done.11, bf16[1024,192]{1,0:T(8,128)(2,1)S(1)} %bitcast.95, bf16[1024,192]{1,0:T(8,128)(2,1)S(1)} %reshape.297), kind=kOutput, calls=%fused_computation.8 | convolution fusion | flops 407895040 | bytes 4994048 | tf_op jit(solution)/shard_map/dot_general | solution.py:31
  72.9 1.9 %fusion.54 = f32[1024]{0:T(1024)S(1)} fusion(f32[1024]{0:T(1024)S(1)} %get-tuple-element.30, f32[1024,1024]{1,0:T(8,128)S(1)} %get-tuple-element.31, s32[1024]{0:T(1024)S(1)} %fusion.33, s32[1024]{0:T(1024)S(1)} %add.265, pred[1024]{0:T(1024)(128)(4,1)S(1)} %copy-done.11), kind=kLoop, calls=%fused_computation.131 | loop fusion | flops 7339008 | bytes 4211712 | tf_op jit(solution)/shard_map/reduce_sum | solution.py:37
  74.8 1.8 %fusion.6 = f32[1024,128]{1,0:T(8,128)S(1)} fusion(bf16[1024,128]{1,0:T(8,128)(2,1)S(1)} %bitcast.96, f32[1024]{0:T(1024)S(1)} %fusion.54, f32[1024,1024]{1,0:T(8,128)S(1)} %get-tuple-element.31, f32[1024]{0:T(1024)S(1)} %get-tuple-element.30, s32[1024]{0:T(1024)S(1)} %fusion.33, s32[1024]{0:T(1024)S(1)} %add.265, pred[1024]{0:T(1024)(128)(4,1)S(1)} %copy-done.11), kind=kOutput, calls=%fused_computation.20 | convolution fusion | flops 275906560 | bytes 4998144 | tf_op jit(solution)/shard_map/dot_general | solution.py:36
  77.8 1.3 %fusion.25 = bf16[64,2048]{1,0:T(8,128)(2,1)} fusion(f32[64,2048]{1,0:T(8,128)S(1)} %reshape.305, f32[8,8,16,128]{3,2,1,0:T(8,128)S(1)} %bitcast.90, f32[64,2048]{1,0:T(8,128)S(1)} %reshape.304, f32[8,8,16,128]{3,2,1,0:T(8,128)S(1)} %bitcast.89, f32[64,2048]{1,0:T(8,128)S(1)} %reshape.298, f32[8,8,16,128]{3,2,1,0:T(8,128)S(1)} %bitcast.88), kind=kLoop, calls=%fused_computation.40 | loop fusion | flops 786432 | bytes 3407872 | tf_op jit(solution)/shard_map/convert_element_type | solution.py:191
  (113 shorter events, 16.7 us)
Async XLA Ops:
  0.0 22.7 %copy-start.1 = (bf16[1024,128]{1,0:T(8,128)(2,1)S(1)}, bf16[1024,128]{1,0:T(8,128)(2,1)}, u32[]{:S(2)}) copy-start(bf16[1024,128]{1,0:T(8,128)(2,1)} %param.12) | copy-start | bytes 786436
  0.0 22.7 %copy-start = (bf16[512,128]{1,0:T(8,128)(2,1)S(1)}, bf16[512,128]{1,0:T(8,128)(2,1)}, u32[]{:S(2)}) copy-start(bf16[512,128]{1,0:T(8,128)(2,1)} %param.14) | copy-start | bytes 393220
  0.0 22.7 %copy-start.7 = (f32[32,192]{1,0:T(8,128)S(1)}, f32[32,192]{1,0:T(8,128)}, u32[]{:S(2)}) copy-start(f32[32,192]{1,0:T(8,128)} %param.15) | copy-start | bytes 73732
  0.0 22.7 %copy-start.8 = (f32[32,128]{1,0:T(8,128)S(1)}, f32[32,128]{1,0:T(8,128)}, u32[]{:S(2)}) copy-start(f32[32,128]{1,0:T(8,128)} %param.16) | copy-start | bytes 49156
  0.0 22.8 %copy-start.3 = (bf16[64,3072]{1,0:T(8,128)(2,1)S(1)}, bf16[64,3072]{1,0:T(8,128)(2,1)}, u32[]{:S(2)}) copy-start(bf16[64,3072]{1,0:T(8,128)(2,1)} %param.10) | copy-start | bytes 1179652
  0.0 25.2 %copy-start.9 = (bf16[64,48]{0,1:T(8,128)(2,1)S(1)}, bf16[64,48]{0,1:T(8,128)(2,1)}, u32[]{:S(2)}) copy-start(bf16[64,48]{0,1:T(8,128)(2,1)} %param.17) | copy-start | bytes 18436
  3.0 36.6 %collective-permute-start = (bf16[16,192]{1,0:T(8,128)(2,1)}, bf16[16,192]{1,0:T(8,128)(2,1)}, u32[]{:S(2)}, u32[]{:S(2)}) collective-permute-start(bf16[16,192]{1,0:T(8,128)(2,1)} %get-tuple-element.13), channel_id=1, source_target_pairs={{0,24},{8,0},{16,8},{24,16},{1,25},{9,1},{17,9},{25,17},{2,26},{10... | collective-permute-start | bytes 18440 | tf_op jit(solution)/shard_map/ppermute | solution.py:18
  8.0 32.5 %collective-permute-start.1 = (bf16[16,192]{1,0:T(8,128)(2,1)}, bf16[16,192]{1,0:T(8,128)(2,1)}, u32[]{:S(2)}, u32[]{:S(2)}) collective-permute-start(bf16[16,192]{1,0:T(8,128)(2,1)} %get-tuple-element.14), channel_id=1, source_target_pairs={{0,24},{8,0},{16,8},{24,16},{1,25},{9,1},{17,9},{25,17},{2,26},{10... | collective-permute-start | bytes 18440 | tf_op jit(solution)/shard_map/ppermute | solution.py:18
  9.8 25.8 %collective-permute-start.2 = (bf16[16,128]{1,0:T(8,128)(2,1)}, bf16[16,128]{1,0:T(8,128)(2,1)}, u32[]{:S(2)}, u32[]{:S(2)}) collective-permute-start(bf16[16,128]{1,0:T(8,128)(2,1)} %get-tuple-element.15), channel_id=1, source_target_pairs={{0,24},{8,0},{16,8},{24,16},{1,25},{9,1},{17,9},{25,17},{2,26},{10... | collective-permute-start | bytes 12296 | tf_op jit(solution)/shard_map/ppermute | solution.py:18
  10.2 28.2 %collective-permute-start.3 = (bf16[16,128]{1,0:T(8,128)(2,1)}, bf16[16,128]{1,0:T(8,128)(2,1)}, u32[]{:S(2)}, u32[]{:S(2)}) collective-permute-start(bf16[16,128]{1,0:T(8,128)(2,1)} %get-tuple-element.16), channel_id=1, source_target_pairs={{0,24},{8,0},{16,8},{24,16},{1,25},{9,1},{17,9},{25,17},{2,26},{10... | collective-permute-start | bytes 12296 | tf_op jit(solution)/shard_map/ppermute | solution.py:18
  13.7 13.6 %all-to-all-start = ((s32[1,4,4]{1,0,2:T(1,128)}), s32[1,4,4]{1,0,2:T(1,128)S(1)}, u32[]{:S(2)}, u32[]{:S(2)}) async-start(s32[1,4,4]{1,0,2:T(1,128)} %copy.85), calls=%async_computation | async-start | bytes 4096 | tf_op jit(solution)/shard_map/all_to_all | solution.py:133
  19.9 41.7 %collective-permute-start.4 = (bf16[256,192]{0,1:T(8,128)(2,1)S(1)}, bf16[256,192]{0,1:T(8,128)(2,1)}, u32[]{:S(2)}, u32[]{:S(2)}) collective-permute-start(bf16[256,192]{0,1:T(8,128)(2,1)S(1)} %slice_select_fusion), channel_id=1, source_target_pairs={{0,8},{8,16},{16,24},{24,0},{1,9},{9,17},{17,25},{25,1},{2,10},{10... | collective-permute-start | bytes 294920 | tf_op jit(solution)/shard_map/ppermute | solution.py:18
  31.1 26.8 %all-to-all-start.2 = ((bf16[1,4,4,64,128]{4,3,1,0,2:T(8,128)(2,1)}), bf16[1,4,4,64,128]{4,3,1,0,2:T(8,128)(2,1)S(1)}, u32[]{:S(2)}, u32[]{:S(2)}) async-start(bf16[1,4,4,64,128]{4,3,1,0,2:T(8,128)(2,1)} %copy.95), calls=%async_computation.2 | async-start | bytes 524288 | tf_op jit(solution)/shard_map/all_to_all | solution.py:151
  35.6 28.0 %collective-permute-start.5 = (bf16[256,128]{1,0:T(8,128)(2,1)S(1)}, bf16[256,128]{1,0:T(8,128)(2,1)}, u32[]{:S(2)}, u32[]{:S(2)}) collective-permute-start(bf16[256,128]{1,0:T(8,128)(2,1)S(1)} %slice_select_fusion.1), channel_id=1, source_target_pairs={{0,8},{8,16},{16,24},{24,0},{1,9},{9,17},{17,25},{25,1},{2,10},{10... | collective-permute-start | bytes 196616 | tf_op jit(solution)/shard_map/ppermute | solution.py:18
  41.4 14.8 %copy-start.10 = (s32[384]{0:T(512)S(1)}, s32[384]{0:T(512)}, u32[]{:S(2)}) copy-start(s32[384]{0:T(512)} %multiply_add_fusion) | copy-start | bytes 4612
  57.8 3.8 %copy-start.2 = (bf16[512,192]{0,1:T(8,128)(2,1)S(1)}, bf16[512,192]{0,1:T(8,128)(2,1)}, u32[]{:S(2)}) copy-start(bf16[512,192]{0,1:T(8,128)(2,1)} %param.13) | copy-start | bytes 589828
  57.9 13.7 %all-to-all-start.1 = ((bf16[1,4,4,64,192]{4,3,1,0,2:T(8,128)(2,1)}), bf16[1,4,4,64,192]{4,3,1,0,2:T(8,128)(2,1)S(1)}, u32[]{:S(2)}, u32[]{:S(2)}) async-start(bf16[1,4,4,64,192]{4,3,1,0,2:T(8,128)(2,1)} %copy_select_fusion), calls=%async_computation.1 | async-start | bytes 1048576 | tf_op jit(solution)/shard_map/all_to_all | solution.py:150
  65.1 6.5 %copy-start.11 = (pred[1024]{0:T(1024)(128)(4,1)S(1)}, pred[1024]{0:T(1024)(128)(4,1)}, u32[]{:S(2)}) copy-start(pred[1024]{0:T(1024)(128)(4,1)} %and.99) | copy-start | bytes 3076
  74.8 2.0 %copy-start.4 = (f32[64,16]{1,0:T(8,128)S(1)}, f32[64,16]{1,0:T(8,128)}, u32[]{:S(2)}) copy-start(f32[64,16]{1,0:T(8,128)} %copy.76) | copy-start | bytes 12292
  76.6 0.8 copy-start.5
  76.6 0.9 %copy-start.6 = (f32[64,16]{1,0:T(8,128)S(1)}, f32[64,16]{1,0:T(8,128)}, u32[]{:S(2)}) copy-start(f32[64,16]{1,0:T(8,128)} %copy.97) | copy-start | bytes 12292
